TPU v7x, 512 devices: a whole 4x4x16 slice. The times are simulated.
512 devices in a mesh: seq: 64 (over z, y), head: 4 (over x), dp: 2 (over core).
Axes of the slice: x: 4, y: 4, z: 16, core: 2. Of those that a mesh axis runs over, the one named last changes fastest.
Arguments:
- queries: bfloat16 [2, 8192, 4096], P('dp', 'seq', 'head'), may hold values from -0.23925781 to 0.23925781
- key_rows: bfloat16 [2, 8192, 4096], P('dp', 'seq', 'head'), may hold values from -0.23925781 to 0.23925781
- values: bfloat16 [2, 8192, 4096], P('dp', 'seq', 'head'), may hold values from -6 to 6
- out_grad: bfloat16 [2, 8192, 4096], P('dp', 'seq', 'head'), may hold values from -6 to 6
- decay_rate: float32 [32], P('head'), may hold values from 4e-05 to 0.025, as said below
- rotation: float32 [4, 4096], P(None, 'head')
- refusal: float32 [4096, 2], P('head')
- proj_weight: float32 [4, 4096], P(None, 'head'), may hold values from -0.09375 to 0.09375
- proj_bias: float32 [4], replicated, may hold values from -4 to 4
- positions: int32 [2, 16], P('dp'), may hold values from 0 to 8191, as said below
Outputs:
- attended: bfloat16 [2, 8192, 4096], P('dp', 'seq', 'head')
- grad_query: bfloat16 [2, 8192, 4096], P('dp', 'seq', 'head')
- grad_key: bfloat16 [2, 8192, 4096], P('dp', 'seq', 'head')
- grad_value: bfloat16 [2, 8192, 4096], P('dp', 'seq', 'head')
- grad_rotation: float32 [4, 4096], P(None, 'head')
- grad_weight: float32 [4, 4096], P(None, 'head')
- grad_bias: float32 [4], replicated
Inputs may be any that keep to these rules, and one draw needn't show every extreme that they name: 16 distinct positions in ascending order; among them always 0, 4096 and 8191. `decay_rate`: one rate per head, the same at every position.
All inputs are finite; a program needn't handle non-finite values.
Results may differ from a plain program's by a relative error of at most 0.0032.
Values sent between devices are 32-bit elements; how exact they have to be, the bound alone decides.
No kernel may reach another device: no remote copies, remote signals or barrier semaphores. Data moves between devices by JAX's collectives and lax.ppermute only.
A program may use at most 128 MiB of HBM per device.

v0:
```python
import jax
import jax.numpy as jnp
from jax import lax
from jax.sharding import PartitionSpec as P

highest = lax.Precision.HIGHEST


def carried_in(x, axis, combine, identity, reverse):
    peers, place = (lax.axis_size(axis), lax.axis_index(axis))
    everything = jax.tree.map(lambda part: lax.all_gather(part, axis), x)
    start = jax.tree.map(
        lambda part, zero: jnp.broadcast_to(jnp.asarray(zero, part.dtype), part.shape), x, identity
    )

    def lap(k, before):
        at = peers - 1 - k if reverse else k
        reached = at > place if reverse else at < place
        new = combine(before, jax.tree.map(lambda part: part[at], everything))
        return jax.tree.map(lambda a, b: jnp.where(reached, a, b), new, before)

    return lax.fori_loop(0, peers, lap, start)


def decay_table(log_decay, count):
    offsets = jnp.arange(count)
    between = offsets[:, None] - offsets[None, :]
    powers = jnp.exp(jnp.maximum(between, 0).astype(jnp.float32)[None] * log_decay[:, None, None])
    return jnp.where(between[None] >= 0, powers, 0.0)


def gram_inverse(gram):
    determinant = gram[0, 0] * gram[1, 1] - gram[0, 1] * gram[1, 0]
    adjugate = jnp.stack(
        [jnp.stack([gram[1, 1], -gram[0, 1]]), jnp.stack([-gram[1, 0], gram[0, 0]])]
    )
    return adjugate / determinant


def chain_combine(earlier, later):
    return (earlier[0] * later[0], later[0][:, None, None] * earlier[1] + later[1])


def shards(
    queries,
    key_rows,
    values,
    out_grad,
    decay_rate,
    rotation,
    refusal,
    proj_weight,
    proj_bias,
    positions,
):
    group = queries.shape[1]
    local_width = queries.shape[2]
    local_heads = decay_rate.shape[0]
    head_size = local_width // local_heads
    query_heads = queries[0].reshape(group, local_heads, head_size)
    key_heads = key_rows[0].reshape(group, local_heads, head_size)
    grad_heads = out_grad[0].reshape(group, local_heads, head_size)
    places = lax.axis_index("seq") * group + jnp.arange(group, dtype=jnp.int32)
    selector = places[:, None] == positions[0][None, :]
    select_low = selector.astype(jnp.bfloat16)
    select_full = selector.astype(jnp.float32)
    picked = jnp.dot(select_low.T, values[0], preferred_element_type=jnp.float32)
    gram_part = jnp.dot(refusal.T, refusal, precision=highest)
    coupling_part = jnp.dot(rotation, refusal, precision=highest)
    gram, coupling = lax.psum((gram_part, coupling_part), "head")
    inverse = gram_inverse(gram)
    rotated = rotation - jnp.dot(
        jnp.dot(coupling, inverse, precision=highest), refusal.T, precision=highest
    )
    code = (
        lax.psum(jnp.dot(picked, (proj_weight - rotated).T, precision=highest), "head") + proj_bias
    )
    shift_rows = jnp.dot(code, rotated, precision=highest)
    moved = (
        values[0].astype(jnp.float32) + jnp.dot(select_full, shift_rows, precision=highest)
    ).astype(jnp.bfloat16)
    moved_heads = moved.reshape(group, local_heads, head_size)
    log_decay = jnp.log1p(-decay_rate)
    table = decay_table(log_decay, group)
    offsets = jnp.arange(group).astype(jnp.float32)
    enter = jnp.exp((offsets + 1.0)[:, None] * log_decay[None, :])
    leave = jnp.exp((group - offsets)[:, None] * log_decay[None, :])
    start_weight = jnp.exp(offsets[:, None] * log_decay[None, :])
    end_weight = jnp.exp((group - 1.0 - offsets)[:, None] * log_decay[None, :])
    keep = jnp.exp(group * log_decay)
    query_full = query_heads.astype(jnp.float32)
    key_full = key_heads.astype(jnp.float32)
    moved_full = moved_heads.astype(jnp.float32)
    grad_full = grad_heads.astype(jnp.float32)
    local_state = jnp.einsum(
        "shd,she->hde", key_full * end_weight[:, :, None], moved_full, precision=highest
    )
    local_grad = jnp.einsum(
        "thd,the->hde", query_full * start_weight[:, :, None], grad_full, precision=highest
    )
    blank = (jnp.ones_like(keep), jnp.zeros_like(local_state))
    entering = carried_in((keep, local_state), "seq", chain_combine, blank, False)[1]
    leaving = carried_in((keep, local_grad), "seq", chain_combine, blank, True)[1]
    scores = jnp.einsum("thd,shd->hts", query_heads, key_heads, preferred_element_type=jnp.float32)
    mixing = (scores * table).astype(jnp.bfloat16)
    inner = jnp.einsum("hts,she->the", mixing, moved_heads, preferred_element_type=jnp.float32)
    outer = enter[:, :, None] * jnp.einsum("thd,hde->the", query_full, entering, precision=highest)
    attended = (inner + outer).astype(jnp.bfloat16).reshape(1, group, local_width)
    grad_scores = jnp.einsum(
        "the,she->hts", grad_heads, moved_heads, preferred_element_type=jnp.float32
    )
    grad_mixing = (grad_scores * table).astype(jnp.bfloat16)
    grad_query = jnp.einsum(
        "hts,shd->thd", grad_mixing, key_heads, preferred_element_type=jnp.float32
    )
    grad_query = grad_query + enter[:, :, None] * jnp.einsum(
        "the,hde->thd", grad_full, entering, precision=highest
    )
    grad_key = jnp.einsum(
        "hts,thd->shd", grad_mixing, query_heads, preferred_element_type=jnp.float32
    )
    grad_key = grad_key + leave[:, :, None] * jnp.einsum(
        "she,hde->shd", moved_full, leaving, precision=highest
    )
    grad_moved = jnp.einsum("hts,the->she", mixing, grad_heads, preferred_element_type=jnp.float32)
    grad_moved = grad_moved + leave[:, :, None] * jnp.einsum(
        "shd,hde->she", key_full, leaving, precision=highest
    )
    grad_moved = grad_moved.reshape(group, local_width)
    picked_grad = jnp.dot(select_full.T, grad_moved, precision=highest)
    code_grad = lax.psum(jnp.dot(picked_grad, rotated.T, precision=highest), "head")
    rotated_grad = jnp.dot(code.T, picked_grad, precision=highest) - jnp.dot(
        code_grad.T, picked, precision=highest
    )
    projected = lax.psum(jnp.dot(rotated_grad, refusal, precision=highest), "head")
    rotation_part = rotated_grad - jnp.dot(
        jnp.dot(projected, inverse, precision=highest), refusal.T, precision=highest
    )
    weight_part = jnp.dot(code_grad.T, picked, precision=highest)
    bias_part = jnp.sum(code_grad, axis=0)
    grad_weight, grad_bias, grad_rotation = lax.psum(
        (weight_part, bias_part, rotation_part), ("seq", "dp")
    )
    value_fix = jnp.dot(code_grad, proj_weight - rotated, precision=highest)
    grad_value = (
        (grad_moved + jnp.dot(select_full, value_fix, precision=highest))
        .astype(jnp.bfloat16)
        .reshape(1, group, local_width)
    )
    grad_query = grad_query.astype(jnp.bfloat16).reshape(1, group, local_width)
    grad_key = grad_key.astype(jnp.bfloat16).reshape(1, group, local_width)
    return (attended, grad_query, grad_key, grad_value, grad_rotation, grad_weight, grad_bias)


def solution(mesh):
    return jax.shard_map(
        shards,
        mesh=mesh,
        in_specs=(
            P("dp", "seq", "head"),
            P("dp", "seq", "head"),
            P("dp", "seq", "head"),
            P("dp", "seq", "head"),
            P("head"),
            P(None, "head"),
            P("head", None),
            P(None, "head"),
            P(),
            P("dp", None),
        ),
        out_specs=(
            P("dp", "seq", "head"),
            P("dp", "seq", "head"),
            P("dp", "seq", "head"),
            P("dp", "seq", "head"),
            P(None, "head"),
            P(None, "head"),
            P(),
        ),
        check_vma=False,
    )
```

profile of v0, /device:TPU:2, one launch (start us, length us, event | category | flops | bytes accessed | tf_op | source)
XLA Modules:
  0.0 1008.6 jit_solution(10857134564750874823)
XLA Ops:
  9.5 1.3 dynamic-slice
  12.3 1.5 fusion.20
  14.9 13.6 %all-reduce.3 = (f32[4,2]{0,1:T(2,128)S(1)}, f32[2,2]{1,0:T(2,128)S(1)}) all-reduce(f32[4,2]{0,1:T(2,128)S(1)} %fusion.63, f32[2,2]{1,0:T(2,128)S(1)} %fusion.64), channel_id=1, replica_groups=mesh['seq'=64,'head'=4,'dp'=2] {'head'}, use_global_device_ids=true, to_apply=%region_0.0 | all-reduce | flops 12 | bytes 96 | tf_op jit(solution)/shard_map/psum | solution.py:70
  31.7 146.4 %all-reduce = f32[512]{0:T(512)S(1)} all-reduce(f32[512]{0:T(512)S(1)} %get-tuple-element.328), channel_id=2, replica_groups=mesh['seq'=64,'head'=4,'dp'=2] {'seq'}, use_global_device_ids=true, to_apply=%add | all-reduce | flops 512 | bytes 4096
  180.8 1.4 maximum_bitcast_fusion
  183.9 1.2 fusion.30
  186.4 127.3 %all-gather.8.cloned.1.call-done = f32[512,128,128]{2,1,0:T(8,128)} async-done(((f32[8,128,128]{2,1,0:T(8,128)}), f32[512,128,128]{2,1,0:T(8,128)}) %all-gather.8.cloned.1.call-update) | async-done | bytes 33554448 | tf_op jit(solution)/shard_map/all_gather | solution.py:11
  313.7 78.5 %while.31 = (s32[]{:T(128)}, f32[8,128,128]{2,1,0:T(8,128)S(1)}, s32[]{:T(128)}, f32[64,8]{1,0:T(8,128)S(1)}, f32[64,8,128,128]{3,2,1,0:T(8,128)}, /*index=5*/s32[]{:T(128)}, s32[]{:T(128)}, s32[]{:T(128)}, s32[]{:T(128)}) while((s32[]{:T(128)}, f32[8,128,128]{2,1,0:T(8,128)S(1)}, s32[]{:T(128)}, f32[64,8]{1,0:T(8,128)S(1)}, ...), condition=%wide.region_6.7_spmd.clone, body=%wide.region_5.6_spmd.clone.sunk | while | flops 524296 | bytes 1573127 | solution.py:22
  314.9 1.2 fusion.114
  316.1 1.2 fusion.114
  317.4 1.2 fusion.114
  318.6 1.2 fusion.114
  319.8 1.2 fusion.114
  321.1 1.2 fusion.114
  322.3 1.2 fusion.114
  324.7 1.2 fusion.114
  333.3 1.2 fusion.114
  341.9 1.2 fusion.114
  348.1 1.2 fusion.114
  356.6 1.2 fusion.114
  365.2 1.2 fusion.114
  371.4 1.2 fusion.114
  380.0 1.2 fusion.114
  388.6 1.2 fusion.114
  394.3 8.6 all-reduce.2
  403.9 1.4 fusion.19
  405.3 1.2 fusion.23
  407.7 10.2 %psum.60 = f32[4,2]{0,1:T(2,128)S(1)} all-reduce(f32[4,2]{0,1:T(2,128)S(1)} %fusion.68), channel_id=1, replica_groups=mesh['seq'=64,'head'=4,'dp'=2] {'head'}, use_global_device_ids=true, to_apply=%region_8.9 | all-reduce | flops 8 | bytes 64 | tf_op jit(solution)/shard_map/psum | solution.py:135
  418.2 1.2 fusion.16
  422.3 495.7 %all-reduce.1 = (f32[4,1024]{1,0:T(4,128)}, f32[4,1024]{1,0:T(4,128)}, f32[4]{0:T(128)}) all-reduce(f32[4,1024]{1,0:T(4,128)S(1)} %convolution_subtract_fusion, f32[4,1024]{1,0:T(4,128)S(1)} %fusion.67, f32[4]{0:T(128)S(1)} %reduce_sum.9), channel_id=1, replica_groups=mesh['seq'=64,'head'=4,'dp'=2] {'seq','dp'}, use_global_device_ids=true, to_apply=%region_9.10 | all-reduce | flops 8196 | bytes 65568 | tf_op jit(solution)/shard_map/psum | solution.py:141
  919.0 1.8 fusion.18
  920.8 77.7 %while.30 = (s32[]{:T(128)}, f32[8,128,128]{2,1,0:T(8,128)S(1)}, s32[]{:T(128)}, f32[64,8]{1,0:T(8,128)S(1)}, f32[64,8,128,128]{3,2,1,0:T(8,128)}, /*index=5*/s32[]{:T(128)}, s32[]{:T(128)}) while((s32[]{:T(128)}, f32[8,128,128]{2,1,0:T(8,128)S(1)}, s32[]{:T(128)}, f32[64,8]{1,0:T(8,128)S(1)}, f32[64,8,128,128]{3,2,1,0:T(8,128)}, ...), condition=%wide.region_4.5_spmd.clone, body=%wide.region_3.4_spmd.clone.sunk | while | flops 524292 | bytes 1573065 | solution.py:22
  (305 shorter events, 153.5 us)
Async XLA Ops:
  7.2 6.7 copy-start
  7.2 306.5 %all-gather.8.cloned.1.call-start = ((), (), s32[]{:S(2)}) async-start(), calls=%async_computation.1 | async-start | bytes 34078720 | tf_op jit(solution)/shard_map/all_gather | solution.py:11
  12.2 301.5 %copy-start.5 = (f32[8]{0:T(128)}, f32[8]{0:T(128)S(1)}, u32[]{:S(2)}) copy-start(f32[8]{0:T(128)S(1)} %get-tuple-element.327) | copy-start | bytes 100
  13.8 907.0 %all-gather.6.cloned.1.call-start = ((), (), s32[]{:S(2)}) async-start(), calls=%async_computation | async-start | bytes 34078720 | tf_op jit(solution)/shard_map/all_gather | solution.py:11
  180.8 237.1 %copy-start.4 = (s32[128]{0:T(128)}, s32[128]{0:T(128)S(1)}, u32[]{:S(2)}) copy-start(s32[128]{0:T(128)S(1)} %iota_add_fusion) | copy-start | bytes 1540
  182.1 0.6 copy-start.6
  182.2 235.7 %copy-start.3 = (pred[128,128]{1,0:T(8,128)(4,1)}, pred[128,128]{1,0:T(8,128)(4,1)S(1)}, u32[]{:S(2)}) copy-start(pred[128,128]{1,0:T(8,128)(4,1)S(1)} %fusion.43) | copy-start | bytes 49156
  182.2 3.8 copy-start.1
  402.9 15.0 %copy-start.2 = (f32[16,4]{0,1:T(4,128)}, f32[16,4]{0,1:T(4,128)S(1)}, u32[]{:S(2)}) copy-start(f32[16,4]{0,1:T(4,128)S(1)} %get-tuple-element.316) | copy-start | bytes 772
Sparse Core Ops, SparseCore 0:
  13.9 299.7 all-gather.7
  406.6 291.8 all-gather.5
where the time goes:
time: 1020 us; the launch traced here: 1010 us
  blocking collectives  674 us (66%)
  other arithmetic  153 us (15%)
  waiting for transfers between devices  127 us (12%)
  matrix products  20.5 us (2%)
  between operations  18.9 us (2%)
    psum x1, blocking collectives, shards(): lax.psum((weight_part, bias_part, rotation_part), ('seq', 'dp'))  496 us
    select_n x128, other arithmetic, lap(): return jax.tree.map(lambda a, b: jnp.where(reached, a, b), new, before)  150 us
    unnamed x1, blocking collectives  146 us
    all_gather x2, waiting for transfers between devices, carried_in(): everything = jax.tree.map(lambda part: lax.all_gather(part, axis), x)  127 us
  transfers between devices with their start and end apart: 2, of which 1 were waited for; matrix products, arithmetic and copies ran while one was open for 2% of the time, Pallas kernels for 0%

commit v1 on v0

--- a/solution.py
+++ b/solution.py
@@ -139,7 +139,7 @@
     weight_part = jnp.dot(code_grad.T, picked, precision=highest)
     bias_part = jnp.sum(code_grad, axis=0)
     grad_weight, grad_bias, grad_rotation = lax.psum(
-        (weight_part, bias_part, rotation_part), ("seq", "dp")
+        lax.psum((weight_part, bias_part, rotation_part), "dp"), "seq"
     )
     value_fix = jnp.dot(code_grad, proj_weight - rotated, precision=highest)
     grad_value = (

time: 1020 us -> 802 us (0.79)
  blocking collectives: 674 us -> 461 us
    psum x1 -> x2, blocking collectives: 496 us -> 283 us  [the longest x1 279 us: shards(): lax.psum(lax.psum((weight_part, bias_part, rotation_part), 'dp'), 'seq')]
where the time goes in v1:
time: 802 us; the launch traced here: 795 us
  blocking collectives  461 us (57%)
  other arithmetic  153 us (19%)
  waiting for transfers between devices  127 us (16%)
  matrix products  20.5 us (3%)
  between operations  18.9 us (2%)
  local copies, waits for them, and re-layouts  9.93 us (1%)
    psum x1, blocking collectives, shards(): lax.psum(lax.psum((weight_part, bias_part, rotation_part), 'dp'), 'seq')  279 us
    select_n x128, other arithmetic, lap(): return jax.tree.map(lambda a, b: jnp.where(reached, a, b), new, before)  150 us
    unnamed x1, blocking collectives  146 us
    all_gather x2, waiting for transfers between devices, carried_in(): everything = jax.tree.map(lambda part: lax.all_gather(part, axis), x)  127 us
  transfers between devices with their start and end apart: 2, of which 1 were waited for; matrix products, arithmetic and copies ran while one was open for 2% of the time, Pallas kernels for 0%

profile of v1, /device:TPU:2, one launch (start us, length us, event | category | flops | bytes accessed | tf_op | source)
XLA Modules:
  0.0 795.4 jit_solution(12641204423661373421)
XLA Ops:
  9.5 1.3 dynamic-slice
  12.3 1.5 fusion.20
  14.9 13.6 %all-reduce.3 = (f32[4,2]{0,1:T(2,128)S(1)}, f32[2,2]{1,0:T(2,128)S(1)}) all-reduce(f32[4,2]{0,1:T(2,128)S(1)} %fusion.63, f32[2,2]{1,0:T(2,128)S(1)} %fusion.64), channel_id=1, replica_groups=mesh['seq'=64,'head'=4,'dp'=2] {'head'}, use_global_device_ids=true, to_apply=%region_0.0 | all-reduce | flops 12 | bytes 96 | tf_op jit(solution)/shard_map/psum | solution.py:70
  31.7 146.4 %all-reduce = f32[512]{0:T(512)S(1)} all-reduce(f32[512]{0:T(512)S(1)} %get-tuple-element.331), channel_id=2, replica_groups=mesh['seq'=64,'head'=4,'dp'=2] {'seq'}, use_global_device_ids=true, to_apply=%add | all-reduce | flops 512 | bytes 4096
  180.8 1.4 maximum_bitcast_fusion
  183.9 1.2 fusion.30
  186.3 127.3 %all-gather.8.cloned.1.call-done = f32[512,128,128]{2,1,0:T(8,128)} async-done(((f32[8,128,128]{2,1,0:T(8,128)}), f32[512,128,128]{2,1,0:T(8,128)}) %all-gather.8.cloned.1.call-update) | async-done | bytes 33554448 | tf_op jit(solution)/shard_map/all_gather | solution.py:11
  313.7 78.5 %while.31 = (s32[]{:T(128)}, f32[8,128,128]{2,1,0:T(8,128)S(1)}, s32[]{:T(128)}, f32[64,8]{1,0:T(8,128)S(1)}, f32[64,8,128,128]{3,2,1,0:T(8,128)}, /*index=5*/s32[]{:T(128)}, s32[]{:T(128)}, s32[]{:T(128)}, s32[]{:T(128)}) while((s32[]{:T(128)}, f32[8,128,128]{2,1,0:T(8,128)S(1)}, s32[]{:T(128)}, f32[64,8]{1,0:T(8,128)S(1)}, ...), condition=%wide.region_6.7_spmd.clone, body=%wide.region_5.6_spmd.clone.sunk | while | flops 524296 | bytes 1573127 | solution.py:22
  314.9 1.2 fusion.114
  316.1 1.2 fusion.114
  317.4 1.2 fusion.114
  318.6 1.2 fusion.114
  319.8 1.2 fusion.114
  321.1 1.2 fusion.114
  326.0 1.2 fusion.114
  332.1 1.2 fusion.114
  340.7 1.2 fusion.114
  349.3 1.2 fusion.114
  355.4 1.2 fusion.114
  364.0 1.2 fusion.114
  372.6 1.2 fusion.114
  378.7 1.2 fusion.114
  387.3 1.2 fusion.114
  394.3 8.6 %all-reduce.2 = (f32[16,4]{0,1:T(4,128)S(1)}, f32[16,4]{0,1:T(4,128)S(1)}) all-reduce(f32[16,4]{0,1:T(4,128)S(1)} %fusion.55, f32[16,4]{0,1:T(4,128)S(1)} %fusion.66), channel_id=1, replica_groups=mesh['seq'=64,'head'=4,'dp'=2] {'head'}, use_global_device_ids=true, to_apply=%region_2.0 | all-reduce | flops 128 | bytes 1024 | tf_op jit(solution)/shard_map/psum | solution.py:76
  403.9 1.4 fusion.19
  405.3 1.2 fusion.23
  407.7 10.2 %psum.81 = f32[4,2]{0,1:T(2,128)S(1)} all-reduce(f32[4,2]{0,1:T(2,128)S(1)} %fusion.68), channel_id=1, replica_groups=mesh['seq'=64,'head'=4,'dp'=2] {'head'}, use_global_device_ids=true, to_apply=%region_8.9 | all-reduce | flops 8 | bytes 64 | tf_op jit(solution)/shard_map/psum | solution.py:135
  418.2 1.2 fusion.16
  422.2 3.5 all-reduce.4
  425.7 279.0 %all-reduce.1 = (f32[4,1024]{1,0:T(4,128)}, f32[4,1024]{1,0:T(4,128)}, f32[4]{0:T(128)}) all-reduce(f32[4,1024]{1,0:T(4,128)S(1)} %get-tuple-element.319, f32[4,1024]{1,0:T(4,128)S(1)} %get-tuple-element.320, f32[4]{0:T(128)S(1)} %get-tuple-element.321), channel_id=1, replica_groups=mesh['seq'=64,'head'=4,'dp'=2] {'seq'}, use_global_device_ids=true, to_apply=%region_10.11 | all-reduce | flops 8196 | bytes 65568 | tf_op jit(solution)/shard_map/psum | solution.py:141
  705.8 1.8 fusion.18
  707.6 77.7 %while.30 = (s32[]{:T(128)}, f32[8,128,128]{2,1,0:T(8,128)S(1)}, s32[]{:T(128)}, f32[64,8]{1,0:T(8,128)S(1)}, f32[64,8,128,128]{3,2,1,0:T(8,128)}, /*index=5*/s32[]{:T(128)}, s32[]{:T(128)}) while((s32[]{:T(128)}, f32[8,128,128]{2,1,0:T(8,128)S(1)}, s32[]{:T(128)}, f32[64,8]{1,0:T(8,128)S(1)}, f32[64,8,128,128]{3,2,1,0:T(8,128)}, ...), condition=%wide.region_4.5_spmd.clone, body=%wide.region_3.4_spmd.clone.sunk | while | flops 524292 | bytes 1573065 | solution.py:22
  (306 shorter events, 154.7 us)
Async XLA Ops:
  7.2 6.7 copy-start
  7.2 306.5 %all-gather.8.cloned.1.call-start = ((), (), s32[]{:S(2)}) async-start(), calls=%async_computation.1 | async-start | bytes 34078720 | tf_op jit(solution)/shard_map/all_gather | solution.py:11
  12.2 301.5 %copy-start.5 = (f32[8]{0:T(128)}, f32[8]{0:T(128)S(1)}, u32[]{:S(2)}) copy-start(f32[8]{0:T(128)S(1)} %get-tuple-element.330) | copy-start | bytes 100
  13.8 693.8 %all-gather.6.cloned.1.call-start = ((), (), s32[]{:S(2)}) async-start(), calls=%async_computation | async-start | bytes 34078720 | tf_op jit(solution)/shard_map/all_gather | solution.py:11
  180.7 237.1 %copy-start.4 = (s32[128]{0:T(128)}, s32[128]{0:T(128)S(1)}, u32[]{:S(2)}) copy-start(s32[128]{0:T(128)S(1)} %iota_add_fusion) | copy-start | bytes 1540
  182.1 0.6 copy-start.6
  182.2 235.7 %copy-start.3 = (pred[128,128]{1,0:T(8,128)(4,1)}, pred[128,128]{1,0:T(8,128)(4,1)S(1)}, u32[]{:S(2)}) copy-start(pred[128,128]{1,0:T(8,128)(4,1)S(1)} %fusion.43) | copy-start | bytes 49156
  182.2 3.8 copy-start.1
  402.9 15.0 %copy-start.2 = (f32[16,4]{0,1:T(4,128)}, f32[16,4]{0,1:T(4,128)S(1)}, u32[]{:S(2)}) copy-start(f32[16,4]{0,1:T(4,128)S(1)} %get-tuple-element.316) | copy-start | bytes 772
Sparse Core Ops, SparseCore 0:
  13.9 299.7 all-gather.7
  406.6 293.5 all-gather.5
